TPU v7x, 32 devices: a whole 2x2x4 slice. The times are simulated.
32 devices in a mesh: space: 8 (over z, x), band: 4 (over y, core).
Axes of the slice: x: 2, y: 2, z: 4, core: 2. Of those that a mesh axis runs over, the one named last changes fastest.
Arguments:
- orbitals: float32 [96, 512, 256], P('space', 'band'), may hold values from -6 to 6
- potential: float32 [96, 256], P('space'), may hold values from -10 to 10
Outputs:
- rotated: float32 [96, 512, 256], P('space', 'band')
- correlation: float32 [512, 512], replicated
All inputs are finite; a program needn't handle non-finite values.
Results may differ from a plain program's by a relative error of at most 0.000098.
Values sent between devices are 32-bit elements; how exact they have to be, the bound alone decides.
A program may use at most 320 MiB of HBM per device.

v0:
```python
import jax
import jax.numpy as jnp
import numpy as np
from jax import lax
from jax.sharding import PartitionSpec as P
from jax.experimental import pallas as pl
from jax.experimental.pallas import tpu as pltpu

EXACT = lax.Precision.HIGHEST
BLOCK = 128
ROWS = 8


def factor_block(tile, spread):
    shape = (ROWS, BLOCK)
    lane = lax.broadcasted_iota(jnp.int32, shape, 1)
    row = lax.broadcasted_iota(jnp.int32, shape, 0)
    groups = BLOCK // ROWS
    for t in range(groups):
        base = t * ROWS
        inside = (lane >= base) & (lane < base + ROWS)
        panel = tile[base : base + ROWS, :]
        below = [tile[g * ROWS : (g + 1) * ROWS, :] for g in range(t + 1, groups)]
        cols = [
            [jnp.broadcast_to(block[:, base + j : base + j + 1], shape) for j in range(ROWS)]
            for block in below
        ]
        for j in range(ROWS):
            spread[j * ROWS : (j + 1) * ROWS, :] = jnp.broadcast_to(
                panel[:, base + j : base + j + 1], shape
            )
        tile[base : base + ROWS, :] = jnp.where(
            inside, jnp.where(lane == base + row, 1.0, 0.0), panel
        )
        below = [jnp.where(inside, 0.0, block) for block in below]
        own = {}
        for j in range(ROWS):
            for i in range(j, ROWS):
                own[i, j] = jnp.broadcast_to(spread[j * ROWS + i : j * ROWS + i + 1, :], shape)
        line = [
            jnp.broadcast_to(tile[base + j : base + j + 1, :], shape) for j in range(ROWS)
        ]
        for j in range(ROWS):
            scale = lax.rsqrt(own[j, j])
            line[j] = line[j] * scale
            for i in range(j + 1, ROWS):
                own[i, j] = own[i, j] * scale
            for i in range(j + 1, ROWS):
                for k in range(j + 1, i + 1):
                    own[i, k] = own[i, k] - own[i, j] * own[k, j]
                line[i] = line[i] - own[i, j] * line[j]
            for g in range(len(below)):
                cols[g][j] = cols[g][j] * scale
                for k in range(j + 1, ROWS):
                    cols[g][k] = cols[g][k] - cols[g][j] * own[k, j]
                below[g] = below[g] - cols[g][j] * line[j]
        for j in range(ROWS):
            tile[base + j : base + j + 1, :] = line[j][0:1, :]
        for g in range(len(below)):
            start = (t + 1 + g) * ROWS
            tile[start : start + ROWS, :] = below[g]


def inverse_factor_kernel(s_ref, w_ref, tile, spread, panel):
    size = s_ref.shape[0]
    blocks = size // BLOCK
    w_ref[...] = s_ref[...]
    lower = lax.broadcasted_iota(jnp.int32, (BLOCK, BLOCK), 0) >= lax.broadcasted_iota(
        jnp.int32, (BLOCK, BLOCK), 1
    )

    def step(k, carry):
        rows = pl.ds(pl.multiple_of(k * BLOCK, BLOCK), BLOCK)
        tile[...] = w_ref[rows, rows]
        factor_block(tile, spread)
        inverse = jnp.where(lower, tile[...], 0.0)
        panel[...] = jnp.dot(
            inverse, w_ref[rows, :], precision=EXACT, preferred_element_type=jnp.float32
        )

        def update(i, carry):
            other = pl.ds(pl.multiple_of(i * BLOCK, BLOCK), BLOCK)
            left = panel[:, other]
            w_ref[other, rows] = jnp.zeros((BLOCK, BLOCK), jnp.float32)
            w_ref[other, :] = w_ref[other, :] - lax.dot_general(
                left,
                panel[...],
                (((0,), (0,)), ((), ())),
                precision=EXACT,
                preferred_element_type=jnp.float32,
            )
            return carry

        keep = [panel[:, c * BLOCK : (c + 1) * BLOCK] for c in range(blocks)]
        for c in range(blocks):
            panel[:, c * BLOCK : (c + 1) * BLOCK] = jnp.where(k == c, inverse, keep[c])
        lax.fori_loop(k + 1, blocks, update, 0)
        w_ref[rows, :] = panel[...]
        return carry

    lax.fori_loop(0, blocks, step, 0)
    for c in range(blocks):
        for r in range(blocks):
            if r < c:
                w_ref[r * BLOCK : (r + 1) * BLOCK, c * BLOCK : (c + 1) * BLOCK] = jnp.zeros(
                    (BLOCK, BLOCK), jnp.float32
                )


def inverse_factor(correlation):
    size = correlation.shape[0]
    return pl.pallas_call(
        inverse_factor_kernel,
        out_shape=jax.ShapeDtypeStruct((size, size), jnp.float32),
        in_specs=[pl.BlockSpec(memory_space=pltpu.VMEM)],
        out_specs=pl.BlockSpec(memory_space=pltpu.VMEM),
        scratch_shapes=[
            pltpu.VMEM((BLOCK, BLOCK), jnp.float32),
            pltpu.VMEM((ROWS * ROWS, BLOCK), jnp.float32),
            pltpu.VMEM((BLOCK, size), jnp.float32),
        ],
        compiler_params=pltpu.CompilerParams(vmem_limit_bytes=32 * 1024 * 1024),
    )(correlation)


COEFS = [12.0 / 7.0, -15.0 / 56.0, 10.0 / 189.0, -1.0 / 112.0, 2.0 / 1925.0, -1.0 / 16632.0]
CENTER_COEF = -5369.0 / 1800.0
INV_SPACING2 = 6.25
SHIFT_MID = 42.0
HALF_SPAN = 38.0
NY = 16


def in_plane_matrix(cells):
    nx = cells // NY
    scale = -0.5 * INV_SPACING2
    full = np.zeros((cells, cells))
    for x in range(nx):
        for y in range(NY):
            at = x * NY + y
            full[at, at] += scale * 3.0 * CENTER_COEF - SHIFT_MID
            for k, coef in enumerate(COEFS):
                for sign in (1, -1):
                    full[((x + sign * (k + 1)) % nx) * NY + y, at] += scale * coef
                    full[x * NY + (y + sign * (k + 1)) % NY, at] += scale * coef
    return full.astype(np.float32)


def padded(block, width, axis):
    count = lax.axis_size(axis)
    forward = [(i, (i + 1) % count) for i in range(count)]
    backward = [(target, source) for source, target in forward]
    low = lax.ppermute(block[-width:], axis, forward)
    high = lax.ppermute(block[:width], axis, backward)
    return jnp.concatenate([low, block, high], axis=0)


def shifted_operator(field, potential, matrix):
    full = padded(field, 6, "space")
    total = full.shape[0]
    out = jnp.einsum("zig,gh->zih", field, matrix, precision=EXACT)
    out = out + potential[:, None, :] * field
    for k in range(6):
        s = k + 1
        pair = full[6 + s : total - 6 + s] + full[6 - s : total - 6 - s]
        out = out + (-0.5 * INV_SPACING2 * COEFS[k]) * pair
    return out


def per_device(orbitals, potential):
    matrix = jnp.asarray(in_plane_matrix(orbitals.shape[2]))
    first = shifted_operator(orbitals, potential, matrix) / HALF_SPAN
    second = 2.0 * shifted_operator(first, potential, matrix) / HALF_SPAN - orbitals
    cells = float(second.shape[0] * lax.axis_size("space") * second.shape[2])
    width = second.shape[1]
    every = lax.all_gather(second, "band", axis=1, tiled=True)
    column_part = jnp.einsum("zig,zjg->ij", every, second, precision=EXACT)
    column_sum = lax.psum(column_part, "space")
    correlation = lax.all_gather(column_sum, "band", axis=1, tiled=True) / cells
    inverse = inverse_factor(correlation)
    own = lax.dynamic_slice_in_dim(inverse, lax.axis_index("band") * width, width, 0)
    rotated = jnp.einsum("zig,ji->zjg", every, own, precision=EXACT)
    return (rotated, correlation)


def solution(mesh):
    return jax.shard_map(
        per_device,
        mesh=mesh,
        in_specs=(P("space", "band", None), P("space", None)),
        out_specs=(P("space", "band", None), P()),
        check_vma=False,
    )
```

profile of v0, /device:TPU:0, one launch (start us, length us, event | category | flops | bytes accessed | tf_op | source)
XLA Modules:
  0.0 279.8 jit_solution(11096160331081551678)
XLA Ops:
  7.2 0.0 all-gather.3.cloned.1.call-start
  7.2 1.9 copy.5
  9.1 0.0 copy-start.2
  9.1 0.0 copy-start.3
  9.1 0.0 copy-start.4
  9.1 0.1 fusion.62
  9.2 6.0 %collective-permute-start = (f32[6,128,256]{1,2,0:T(8,128)S(1)}, f32[6,128,256]{1,2,0:T(8,128)S(1)}, u32[]{:S(2)}, u32[]{:S(2)}) collective-permute-start(f32[6,128,256]{1,2,0:T(8,128)S(1)} %get-tuple-element.4), channel_id=1, source_target_pairs={{4,0},{8,4},{12,8},{16,12},{20,16},{24,20},{28,24},{0,28},{5,1},{9... | collective-permute-start | bytes 2359304 | tf_op jit(solution)/shard_map/ppermute | solution.py:154
  15.3 0.0 collective-permute-start.1
  15.3 31.4 %collective-permute-done = f32[6,128,256]{1,2,0:T(8,128)S(1)} collective-permute-done((f32[6,128,256]{1,2,0:T(8,128)S(1)}, f32[6,128,256]{1,2,0:T(8,128)S(1)}, u32[]{:S(2)}, u32[]{:S(2)}) %collective-permute-start) | collective-permute-done | bytes 786464 | tf_op jit(solution)/shard_map/ppermute | solution.py:154
  46.6 0.2 collective-permute-done.1
  46.8 0.0 copy-done.2
  46.8 0.0 copy-done.3
  46.8 0.0 copy-done.4
  46.8 2.6 broadcast_multiply_fusion
  49.4 0.1 fusion.61
  49.5 4.9 %collective-permute-start.2 = (f32[6,128,256]{1,2,0:T(8,128)S(1)}, f32[6,128,256]{1,2,0:T(8,128)S(1)}, u32[]{:S(2)}, u32[]{:S(2)}) collective-permute-start(f32[6,128,256]{1,2,0:T(8,128)S(1)} %get-tuple-element.2), channel_id=1, source_target_pairs={{4,0},{8,4},{12,8},{16,12},{20,16},{24,20},{28,24},{0,28},{5,1},{9... | collective-permute-start | bytes 2359304 | tf_op jit(solution)/shard_map/ppermute | solution.py:154
  54.5 0.0 collective-permute-start.3
  54.5 32.2 %collective-permute-done.2 = f32[6,128,256]{1,2,0:T(8,128)S(1)} collective-permute-done((f32[6,128,256]{1,2,0:T(8,128)S(1)}, f32[6,128,256]{1,2,0:T(8,128)S(1)}, u32[]{:S(2)}, u32[]{:S(2)}) %collective-permute-start.2) | collective-permute-done | bytes 786464 | tf_op jit(solution)/shard_map/ppermute | solution.py:154
  86.6 0.2 collective-permute-done.3
  86.8 8.3 %fusion.6 = f32[12,128,256]{1,2,0:T(8,128)} fusion(f32[12,128,256]{1,2,0:T(8,128)S(1)} %copy.5, f32[12,128,256]{1,2,0:T(8,128)S(1)} %get-tuple-element.6, f32[6,128,256]{1,2,0:T(8,128)S(1)} %collective-permute-done.3, f32[6,128,256]{1,2,0:T(8,128)S(1)} %collective-permute-done.2, f32[12,128,256]{1,2,0:T(8,128)S(1)} %get-tuple-element.7, ...), kind=kOutput, calls=%fused_computation.46 | convolution fusion | flops 1221328896 | bytes 9715712 | tf_op jit(solution)/shard_map/zig,gh->zih/dot_general | solution.py:161
  95.1 0.0 copy-start.1
  95.1 0.0 all-gather.3.cloned.1.call-update
  95.1 0.0 all-reduce.2.cloned.1.call-start
  95.2 47.2 %all-gather.3.cloned.1.call-done = f32[12,512,256]{1,2,0:T(8,128)} async-done(((f32[12,128,256]{1,2,0:T(8,128)}), f32[12,512,256]{1,2,0:T(8,128)}) %all-gather.3.cloned.1.call-update) | async-done | bytes 6291472 | tf_op jit(solution)/shard_map/all_gather | solution.py:176
  142.4 0.0 copy-done.1
  142.4 12.7 %convolution_bitcast_fusion.1 = f32[512,128]{1,0:T(8,128)} fusion(f32[12,512,256]{1,2,0:T(8,128)} %all-gather.3.cloned.1.call-done, f32[12,128,256]{1,2,0:T(8,128)S(1)} %copy-done.1), kind=kOutput, calls=%fused_computation.104 | convolution fusion | flops 2415919104 | bytes 8126464 | tf_op jit(solution)/shard_map/zig,zjg->ij/dot_general | solution.py:177
  155.1 0.0 all-reduce.2.cloned.1.call-update
  155.1 0.2 all-gather.5.cloned.1.call-start
  155.3 70.5 %all-reduce.2.cloned.1.call-done = f32[512,128]{1,0:T(8,128)} async-done(((f32[512,128]{1,0:T(8,128)}), f32[512,128]{1,0:T(8,128)}) %all-reduce.2.cloned.1.call-update) | async-done | bytes 262160 | tf_op jit(solution)/shard_map/psum | solution.py:178
  225.8 0.0 all-gather.5.cloned.1.call-update
  225.8 17.8 %all-gather.5.cloned.1.call-done = f32[512,512]{1,0:T(8,128)} async-done(((f32[512,128]{1,0:T(8,128)}), f32[512,512]{1,0:T(8,128)}) %all-gather.5.cloned.1.call-update) | async-done | bytes 1048592 | tf_op jit(solution)/shard_map/all_gather | solution.py:179
  243.6 1.3 broadcast_multiply_fusion.1.s_ref
  244.9 0.0 copy-start
  244.9 18.0 %shard_map.50 = f32[512,512]{1,0:T(8,128)S(1)} custom-call(f32[512,512]{1,0:T(8,128)S(1)} %broadcast_multiply_fusion.1.s_ref), custom_call_target="tpu_custom_call" | custom-call | tf_op jit(solution)/shard_map/pallas_call | solution.py:112
  262.9 10.3 %convolution_bitcast_fusion = f32[12,128,256]{2,1,0:T(8,128)} fusion(f32[12,512,256]{1,2,0:T(8,128)} %all-gather.3.cloned.1.call-done, f32[512,512]{1,0:T(8,128)S(1)} %shard_map.50, s32[]{:T(128)S(6)} %select_n.3), kind=kOutput, calls=%fused_computation.103 | convolution fusion | flops 2415919104 | bytes 8126468 | tf_op jit(solution)/shard_map/zig,ji->zjg/dot_general | solution.py:182
  273.2 0.0 copy-done
  (1 shorter events, 0.0 us)
Async XLA Ops:
  7.2 135.2 %all-gather.3.cloned.1.call-start = ((), (), s32[]{:S(2)}) async-start(), calls=%async_computation | async-start | bytes 7864320 | tf_op jit(solution)/shard_map/all_gather | solution.py:176
  9.1 37.7 %copy-start.2 = (f32[12,128,256]{2,1,0:T(8,128)S(1)}, f32[12,128,256]{2,1,0:T(8,128)}, u32[]{:S(2)}) copy-start(f32[12,128,256]{2,1,0:T(8,128)} %param.3) | copy-start | bytes 4718596
  9.1 37.7 %copy-start.3 = (f32[12,256]{1,0:T(8,128)S(1)}, f32[12,256]{1,0:T(8,128)}, u32[]{:S(2)}) copy-start(f32[12,256]{1,0:T(8,128)} %param.4) | copy-start | bytes 36868
  9.1 37.7 %copy-start.4 = (f32[256,256,1]{0,1,2:T(8,128)S(1)}, f32[256,256,1]{0,1,2:T(8,128)}, u32[]{:S(2)}) copy-start(f32[256,256,1]{0,1,2:T(8,128)} %constant.37) | copy-start | bytes 786436
  9.2 37.4 %collective-permute-start = (f32[6,128,256]{1,2,0:T(8,128)S(1)}, f32[6,128,256]{1,2,0:T(8,128)S(1)}, u32[]{:S(2)}, u32[]{:S(2)}) collective-permute-start(f32[6,128,256]{1,2,0:T(8,128)S(1)} %get-tuple-element.4), channel_id=1, source_target_pairs={{4,0},{8,4},{12,8},{16,12},{20,16},{24,20},{28,24},{0,28},{5,1},{9... | collective-permute-start | bytes 2359304 | tf_op jit(solution)/shard_map/ppermute | solution.py:154
  15.3 31.5 %collective-permute-start.1 = (f32[6,128,256]{1,2,0:T(8,128)S(1)}, f32[6,128,256]{1,2,0:T(8,128)S(1)}, u32[]{:S(2)}, u32[]{:S(2)}) collective-permute-start(f32[6,128,256]{1,2,0:T(8,128)S(1)} %get-tuple-element.5), channel_id=1, source_target_pairs={{0,4},{4,8},{8,12},{12,16},{16,20},{20,24},{24,28},{28,0},{1,5},{5... | collective-permute-start | bytes 2359304 | tf_op jit(solution)/shard_map/ppermute | solution.py:153
  49.5 37.1 %collective-permute-start.2 = (f32[6,128,256]{1,2,0:T(8,128)S(1)}, f32[6,128,256]{1,2,0:T(8,128)S(1)}, u32[]{:S(2)}, u32[]{:S(2)}) collective-permute-start(f32[6,128,256]{1,2,0:T(8,128)S(1)} %get-tuple-element.2), channel_id=1, source_target_pairs={{4,0},{8,4},{12,8},{16,12},{20,16},{24,20},{28,24},{0,28},{5,1},{9... | collective-permute-start | bytes 2359304 | tf_op jit(solution)/shard_map/ppermute | solution.py:154
  54.5 32.3 %collective-permute-start.3 = (f32[6,128,256]{1,2,0:T(8,128)S(1)}, f32[6,128,256]{1,2,0:T(8,128)S(1)}, u32[]{:S(2)}, u32[]{:S(2)}) collective-permute-start(f32[6,128,256]{1,2,0:T(8,128)S(1)} %get-tuple-element.3), channel_id=1, source_target_pairs={{0,4},{4,8},{8,12},{12,16},{16,20},{20,24},{24,28},{28,0},{1,5},{5... | collective-permute-start | bytes 2359304 | tf_op jit(solution)/shard_map/ppermute | solution.py:153
  95.1 47.3 %copy-start.1 = (f32[12,128,256]{1,2,0:T(8,128)S(1)}, f32[12,128,256]{1,2,0:T(8,128)}, u32[]{:S(2)}) copy-start(f32[12,128,256]{1,2,0:T(8,128)} %fusion.6) | copy-start | bytes 4718596
  95.1 130.7 %all-reduce.2.cloned.1.call-start = ((), (), s32[]{:S(2)}) async-start(), calls=%async_computation.1 | async-start | bytes 524288 | tf_op jit(solution)/shard_map/psum | solution.py:178
  155.1 88.5 %all-gather.5.cloned.1.call-start = ((), (), s32[]{:S(2)}) async-start(), calls=%async_computation.2 | async-start | bytes 1310720 | tf_op jit(solution)/shard_map/all_gather | solution.py:179
  244.9 28.3 %copy-start = (f32[512,512]{1,0:T(8,128)}, f32[512,512]{1,0:T(8,128)S(1)}, u32[]{:S(2)}) copy-start(f32[512,512]{1,0:T(8,128)S(1)} %broadcast_multiply_fusion.1.s_ref) | copy-start | bytes 3145732
Sparse Core Ops, SparseCore 0:
  95.2 47.0 all-gather.2
  155.2 70.5 all-reduce.1
  227.4 16.1 all-gather.4
where the time goes:
time: 280 us
  waiting for transfers between devices  199 us (71%)
  matrix products  33.9 us (12%)
  Pallas kernels  18 us (6%)
  between operations  13.8 us (5%)
  starting transfers between devices  11.3 us (4%)
    psum x1, waiting for transfers between devices, per_device(): column_sum = lax.psum(column_part, 'space')  70.5 us
    ppermute x2, waiting for transfers between devices, padded(): high = lax.ppermute(block[:width], axis, backward)  63.5 us
    all_gather x1, waiting for transfers between devices, per_device(): every = lax.all_gather(second, 'band', axis=1, tiled=True)  47.2 us
    pallas_call x1, Pallas kernels, inverse_factor(): pl.pallas_call(inverse_factor_kernel, out_shape=jax.ShapeDtypeStruct((siz...  18 us
    all_gather x1, waiting for transfers between devices, per_device(): correlation = lax.all_gather(column_sum, 'band', axis=1, tiled=True) / cells  17.8 us
    dot_general x1, matrix products, per_device(): column_part = jnp.einsum('zig,zjg->ij', every, second, precision=EXACT)  12.7 us
    ppermute x2, starting transfers between devices, padded(): high = lax.ppermute(block[:width], axis, backward)  11 us
    dot_general x2, matrix products, shifted_operator(): out = jnp.einsum('zig,gh->zih', field, matrix, precision=EXACT)  10.9 us
  transfers between devices with their start and end apart: 7, of which 7 were waited for; matrix products, arithmetic and copies ran while one was open for 0% of the time, Pallas kernels for 0%

commit v1 on v0

v1 whole, which is shorter than its diff:
```python
import functools
import jax
import jax.numpy as jnp
import numpy as np
from jax import lax
from jax.sharding import PartitionSpec as P
from jax.experimental import pallas as pl
from jax.experimental.pallas import tpu as pltpu

EXACT = lax.Precision.HIGHEST
BLOCK = 128
ROWS = 8


def factor_block(tile, spread):
    shape = (ROWS, BLOCK)
    lane = lax.broadcasted_iota(jnp.int32, shape, 1)
    row = lax.broadcasted_iota(jnp.int32, shape, 0)
    groups = BLOCK // ROWS
    for t in range(groups):
        base = t * ROWS
        inside = (lane >= base) & (lane < base + ROWS)
        panel = tile[base : base + ROWS, :]
        below = [tile[g * ROWS : (g + 1) * ROWS, :] for g in range(t + 1, groups)]
        cols = [
            [jnp.broadcast_to(block[:, base + j : base + j + 1], shape) for j in range(ROWS)]
            for block in below
        ]
        for j in range(ROWS):
            spread[j * ROWS : (j + 1) * ROWS, :] = jnp.broadcast_to(
                panel[:, base + j : base + j + 1], shape
            )
        tile[base : base + ROWS, :] = jnp.where(
            inside, jnp.where(lane == base + row, 1.0, 0.0), panel
        )
        below = [jnp.where(inside, 0.0, block) for block in below]
        own = {}
        for j in range(ROWS):
            for i in range(j, ROWS):
                own[i, j] = jnp.broadcast_to(spread[j * ROWS + i : j * ROWS + i + 1, :], shape)
        line = [
            jnp.broadcast_to(tile[base + j : base + j + 1, :], shape) for j in range(ROWS)
        ]
        for j in range(ROWS):
            scale = lax.rsqrt(own[j, j])
            line[j] = line[j] * scale
            for i in range(j + 1, ROWS):
                own[i, j] = own[i, j] * scale
            for i in range(j + 1, ROWS):
                for k in range(j + 1, i + 1):
                    own[i, k] = own[i, k] - own[i, j] * own[k, j]
                line[i] = line[i] - own[i, j] * line[j]
            for g in range(len(below)):
                cols[g][j] = cols[g][j] * scale
                for k in range(j + 1, ROWS):
                    cols[g][k] = cols[g][k] - cols[g][j] * own[k, j]
                below[g] = below[g] - cols[g][j] * line[j]
        for j in range(ROWS):
            tile[base + j : base + j + 1, :] = line[j][0:1, :]
        for g in range(len(below)):
            start = (t + 1 + g) * ROWS
            tile[start : start + ROWS, :] = below[g]

COEFS = [12.0 / 7.0, -15.0 / 56.0, 10.0 / 189.0, -1.0 / 112.0, 2.0 / 1925.0, -1.0 / 16632.0]
CENTER_COEF = -5369.0 / 1800.0
INV_SPACING2 = 6.25
SHIFT_MID = 42.0
HALF_SPAN = 38.0
NY = 16
REACH = 6
CHUNK = 16
MESH = pl.DeviceIdType.MESH


def in_plane_matrix(cells):
    nx = cells // NY
    scale = -0.5 * INV_SPACING2
    full = np.zeros((cells, cells))
    for x in range(nx):
        for y in range(NY):
            at = x * NY + y
            full[at, at] += scale * 3.0 * CENTER_COEF - SHIFT_MID
            for k, coef in enumerate(COEFS):
                for sign in (1, -1):
                    full[((x + sign * (k + 1)) % nx) * NY + y, at] += scale * coef
                    full[x * NY + (y + sign * (k + 1)) % NY, at] += scale * coef
    return full.astype(np.float32)


def inverse_factor_in(s_ref, w_ref, tile, spread, panel):
    size = s_ref.shape[0]
    blocks = size // BLOCK
    w_ref[...] = s_ref[...]
    lower = lax.broadcasted_iota(jnp.int32, (BLOCK, BLOCK), 0) >= lax.broadcasted_iota(
        jnp.int32, (BLOCK, BLOCK), 1
    )

    def step(k, carry):
        rows = pl.ds(pl.multiple_of(k * BLOCK, BLOCK), BLOCK)
        tile[...] = w_ref[rows, rows]
        factor_block(tile, spread)
        inverse = jnp.where(lower, tile[...], 0.0)
        panel[...] = jnp.dot(
            inverse, w_ref[rows, :], precision=EXACT, preferred_element_type=jnp.float32
        )

        def update(i, carry):
            other = pl.ds(pl.multiple_of(i * BLOCK, BLOCK), BLOCK)
            left = panel[:, other]
            w_ref[other, rows] = jnp.zeros((BLOCK, BLOCK), jnp.float32)
            w_ref[other, :] = w_ref[other, :] - lax.dot_general(
                left,
                panel[...],
                (((0,), (0,)), ((), ())),
                precision=EXACT,
                preferred_element_type=jnp.float32,
            )
            return carry

        keep = [panel[:, c * BLOCK : (c + 1) * BLOCK] for c in range(blocks)]
        for c in range(blocks):
            panel[:, c * BLOCK : (c + 1) * BLOCK] = jnp.where(k == c, inverse, keep[c])
        lax.fori_loop(k + 1, blocks, update, 0)
        w_ref[rows, :] = panel[...]
        return carry

    lax.fori_loop(0, blocks, step, 0)
    for c in range(blocks):
        for r in range(blocks):
            if r < c:
                w_ref[r * BLOCK : (r + 1) * BLOCK, c * BLOCK : (c + 1) * BLOCK] = jnp.zeros(
                    (BLOCK, BLOCK), jnp.float32
                )


def filter_kernel(
    n, nb, cells, o_ref, p_ref, m_ref, every_out, corr_out,
    ext, pot, first, mixed, every, part, inbox, corr,
    own_sem, pot_send, pot_recv, near_send, near_recv, far_send, far_recv,
    chip_send, chip_recv, core_send, core_recv, pass_send, pass_recv,
    rs_send, rs_recv, ag_send, ag_recv,
    cchip_send, cchip_recv, ccore_send, ccore_recv, cpass_send, cpass_recv, out_sem,
):
    nz, width, area = o_ref.shape
    chunks = width // CHUNK
    chips = nb // 2
    s = lax.axis_index("space")
    b = lax.axis_index("band")
    odd = lax.rem(s, 2)
    near = s + 1 - 2 * odd
    far = lax.rem(s + 2 - 4 * odd + n, n)
    chip = b // 2
    core = lax.rem(b, 2)
    mate = b + 1 - 2 * core
    near_slot = 2 * nz * (1 - odd)
    far_slot = 2 * nz * odd

    def space_at(d):
        return lax.rem(s + d + n, n)

    def band_at(d):
        return lax.rem(chip + d + chips, chips) * 2 + core

    barrier = pltpu.get_barrier_semaphore()
    for d in range(1, n):
        pl.semaphore_signal(barrier, inc=1, device_id={"space": space_at(d)}, device_id_type=MESH)
    for d in range(1, chips):
        pl.semaphore_signal(barrier, inc=1, device_id={"band": band_at(d)}, device_id_type=MESH)
    pl.semaphore_signal(barrier, inc=1, device_id={"band": mate}, device_id_type=MESH)
    pl.semaphore_wait(barrier, n - 1 + chips)

    def remote(src, dst, send, recv, target):
        return pltpu.make_async_remote_copy(
            src_ref=src, dst_ref=dst, send_sem=send, recv_sem=recv,
            device_id=target, device_id_type=MESH,
        )

    def rows_of(c):
        return pl.ds(pl.multiple_of(c * CHUNK, CHUNK), CHUNK)

    def near_copy(c):
        return remote(
            o_ref.at[:, rows_of(c), :],
            ext.at[pl.ds(2 * nz * odd, nz), rows_of(c), :],
            near_send.at[c], near_recv.at[c], {"space": near},
        )

    def near_arrival(c):
        spot = ext.at[pl.ds(near_slot, nz), rows_of(c), :]
        return remote(spot, spot, near_send.at[c], near_recv.at[c], {"space": near})

    def far_copy(c):
        return remote(
            ext.at[pl.ds(near_slot, nz), rows_of(c), :],
            ext.at[pl.ds(far_slot, nz), rows_of(c), :],
            far_send.at[c], far_recv.at[c], {"space": far},
        )

    def far_arrival(c):
        spot = ext.at[pl.ds(far_slot, nz), rows_of(c), :]
        return remote(spot, spot, far_send.at[c], far_recv.at[c], {"space": far})

    def block_rows(band, c):
        return pl.ds(pl.multiple_of(band * width + c * CHUNK, CHUNK), CHUNK)

    def chip_copy(d, c):
        spot = every.at[:, block_rows(b, c), :]
        return remote(spot, spot, chip_send.at[d - 1, c], chip_recv.at[d - 1, c], {"band": band_at(d)})

    def core_copy(c):
        spot = every.at[:, block_rows(b, c), :]
        return remote(spot, spot, core_send.at[c], core_recv.at[c], {"band": mate})

    def core_arrival(c):
        spot = every.at[:, block_rows(mate, c), :]
        return remote(spot, spot, core_send.at[c], core_recv.at[c], {"band": mate})

    def pass_copy(d, c):
        spot = every.at[:, block_rows(band_at(-d), c), :]
        return remote(spot, spot, pass_send.at[d - 1, c], pass_recv.at[d - 1, c], {"band": mate})

    def chip_arrival(d, c):
        spot = every.at[:, block_rows(band_at(-d), c), :]
        return remote(spot, spot, chip_send.at[d - 1, c], chip_recv.at[d - 1, c], {"band": band_at(-d)})

    def pass_arrival(d, c):
        other = band_at(-d) + 1 - 2 * core
        spot = every.at[:, block_rows(other, c), :]
        return remote(spot, spot, pass_send.at[d - 1, c], pass_recv.at[d - 1, c], {"band": mate})

    def take_chip(c):
        for d in range(1, chips):
            chip_arrival(d, c).wait_recv()
            pass_copy(d, c).start()

    near_copy(0).start()
    if chunks > 1:
        near_copy(1).start()
    own = pltpu.make_async_copy(o_ref, ext.at[pl.ds(nz, nz)], own_sem)
    own.start()
    up = remote(p_ref, pot.at[pl.ds(0, nz)], pot_send.at[0], pot_recv.at[0], {"space": space_at(1)})
    down = remote(p_ref, pot.at[pl.ds(2 * nz, nz)], pot_send.at[1], pot_recv.at[1], {"space": space_at(-1)})
    up.start()
    down.start()
    pot[nz : 2 * nz] = p_ref[...]

    near_arrival(0).wait_recv()
    far_copy(0).start()
    near_copy(0).wait_send()
    if chunks > 2:
        near_copy(2).start()
    own.wait()
    up.wait_recv()
    down.wait_recv()

    along = [-0.5 * INV_SPACING2 * coef for coef in COEFS]

    def do_chunk(c, carry):
        rows = rows_of(c)

        @pl.when(c + 1 < chunks)
        def _():
            near_arrival(c + 1).wait_recv()
            far_copy(c + 1).start()
            near_copy(c + 1).wait_send()

        @pl.when(c + 3 < chunks)
        def _():
            near_copy(c + 3).start()

        far_arrival(c).wait_recv()

        wide = nz + 2 * REACH
        slab = ext[nz - REACH : 2 * nz + REACH, rows, :].reshape(wide * CHUNK, area)
        mixed[...] = jnp.dot(
            slab, m_ref[...], precision=EXACT, preferred_element_type=jnp.float32
        ).reshape(wide, CHUNK, area)

        def first_plane(f, carry):
            q = f + (nz - REACH)
            total = mixed[f] + pot[q] * ext[q, rows, :]
            for k in range(REACH):
                total = total + along[k] * (ext[q + k + 1, rows, :] + ext[q - k - 1, rows, :])
            first[f] = total * (1.0 / HALF_SPAN)
            return carry

        lax.fori_loop(0, wide, first_plane, 0, unroll=4)

        slab = first[REACH : nz + REACH].reshape(nz * CHUNK, area)
        mixed[0:nz] = jnp.dot(
            slab, m_ref[...], precision=EXACT, preferred_element_type=jnp.float32
        ).reshape(nz, CHUNK, area)

        def second_plane(j, carry):
            f = j + REACH
            total = mixed[j] + pot[j + nz] * first[f]
            for k in range(REACH):
                total = total + along[k] * (first[f + k + 1] + first[f - k - 1])
            every[j, block_rows(b, c), :] = total * (2.0 / HALF_SPAN) - ext[j + nz, rows, :]
            return carry

        lax.fori_loop(0, nz, second_plane, 0, unroll=4)

        for d in range(1, chips):
            chip_copy(d, c).start()
        core_copy(c).start()

        @pl.when(c >= 2)
        def _():
            take_chip(c - 2)

        return carry

    lax.fori_loop(0, chunks, do_chunk, 0)
    if chunks > 1:
        take_chip(chunks - 2)

    def each_chunk(action):
        def run(c, carry):
            action(c)
            return carry

        lax.fori_loop(0, chunks, run, 0)

    total_cols = nb * width
    slice_rows = width // n

    def gram(start, cols):
        def add(z, total):
            mine = every[z, pl.ds(pl.multiple_of(b * width, width), width), :]
            theirs = every[z, pl.ds(start, cols), :]
            return total + lax.dot_general(
                mine, theirs, (((1,), (1,)), ((), ())),
                precision=EXACT, preferred_element_type=jnp.float32,
            )

        total = lax.fori_loop(0, nz, add, jnp.zeros((width, cols), jnp.float32))
        for t in range(n):
            part[t, :, pl.ds(start, cols)] = total[t * slice_rows : (t + 1) * slice_rows, :]

    span = 2 * width
    staged = span % 128 == 0
    each_chunk(lambda c: core_arrival(c).wait_recv())
    if staged:
        gram(pl.multiple_of(chip * span, span), span)
    take_chip(chunks - 1)
    for d in range(1, chips):
        each_chunk(lambda c: pass_arrival(d, c).wait_recv())
        if staged:
            gram(pl.multiple_of(lax.rem(chip - d + chips, chips) * span, span), span)
    if not staged:
        gram(0, total_cols)
    save = pltpu.make_async_copy(every, every_out, out_sem.at[0])
    save.start()

    def rs_copy(d):
        t = space_at(d)
        return remote(part.at[t], inbox.at[d], rs_send.at[d], rs_recv.at[d], {"space": t})

    def ag_copy(d):
        spot = corr.at[b, s]
        return remote(spot, spot, ag_send.at[d], ag_recv.at[d], {"space": space_at(d)})

    def ag_arrival(d):
        spot = corr.at[b, space_at(-d)]
        return remote(spot, spot, ag_send.at[d], ag_recv.at[d], {"space": space_at(d)})

    for d in range(1, n):
        rs_copy(d).start()
    total = part[s]
    for d in range(1, n):
        rs_copy(d).wait_recv()
        total = total + inbox[d]
    corr[b, s] = total / cells
    for d in range(1, n):
        ag_copy(d).start()
    for d in range(1, n):
        ag_arrival(d).wait_recv()

    def cchip_copy(d):
        spot = corr.at[b]
        return remote(spot, spot, cchip_send.at[d - 1], cchip_recv.at[d - 1], {"band": band_at(d)})

    def cchip_arrival(d):
        spot = corr.at[band_at(-d)]
        return remote(spot, spot, cchip_send.at[d - 1], cchip_recv.at[d - 1], {"band": band_at(-d)})

    def cpass_copy(d):
        spot = corr.at[band_at(-d)]
        return remote(spot, spot, cpass_send.at[d - 1], cpass_recv.at[d - 1], {"band": mate})

    def cpass_arrival(d):
        spot = corr.at[band_at(-d) + 1 - 2 * core]
        return remote(spot, spot, cpass_send.at[d - 1], cpass_recv.at[d - 1], {"band": mate})

    ccore = remote(corr.at[b], corr.at[b], ccore_send, ccore_recv, {"band": mate})
    ccore_arrival = remote(corr.at[mate], corr.at[mate], ccore_send, ccore_recv, {"band": mate})
    for d in range(1, chips):
        cchip_copy(d).start()
    ccore.start()
    for d in range(1, chips):
        cchip_arrival(d).wait_recv()
        cpass_copy(d).start()
    ccore_arrival.wait_recv()
    for d in range(1, chips):
        cpass_arrival(d).wait_recv()
    store = pltpu.make_async_copy(corr, corr_out, out_sem.at[1])
    store.start()

    up.wait_send()
    down.wait_send()
    each_chunk(lambda c: far_copy(c).wait_send())
    each_chunk(lambda c: core_copy(c).wait_send())
    for d in range(1, chips):
        each_chunk(lambda c: chip_copy(d, c).wait_send())
        each_chunk(lambda c: pass_copy(d, c).wait_send())
        cchip_copy(d).wait_send()
        cpass_copy(d).wait_send()
    for d in range(1, n):
        rs_copy(d).wait_send()
        ag_copy(d).wait_send()
    ccore.wait_send()
    save.wait()
    store.wait()


def filter_and_correlate(orbitals, potential):
    nz, width, area = orbitals.shape
    n = lax.axis_size("space")
    nb = lax.axis_size("band")
    chunks = width // CHUNK
    chips = nb // 2
    slices = (nb, n, width // n, nb * width)
    dma = pltpu.SemaphoreType.DMA
    f32 = jnp.float32
    hops = max(chips - 1, 1)
    flops = 6 * 2 * nz * width * area * (3 * area + nb * width)
    every, corr = pl.pallas_call(
        functools.partial(filter_kernel, n, nb, float(nz * n * area)),
        out_shape=(
            jax.ShapeDtypeStruct((nz, nb * width, area), f32),
            jax.ShapeDtypeStruct(slices, f32),
        ),
        in_specs=[
            pl.BlockSpec(memory_space=pl.ANY),
            pl.BlockSpec(memory_space=pltpu.VMEM),
            pl.BlockSpec(memory_space=pltpu.VMEM),
        ],
        out_specs=(pl.BlockSpec(memory_space=pl.ANY), pl.BlockSpec(memory_space=pl.ANY)),
        scratch_shapes=[
            pltpu.VMEM((3 * nz, width, area), f32),
            pltpu.VMEM((3 * nz, 1, area), f32),
            pltpu.VMEM((nz + 2 * REACH, CHUNK, area), f32),
            pltpu.VMEM((nz + 2 * REACH, CHUNK, area), f32),
            pltpu.VMEM((nz, nb * width, area), f32),
            pltpu.VMEM(slices[1:], f32),
            pltpu.VMEM(slices[1:], f32),
            pltpu.VMEM(slices, f32),
            dma, dma((2,)), dma((2,)),
            dma((chunks,)), dma((chunks,)), dma((chunks,)), dma((chunks,)),
            dma((hops, chunks)), dma((hops, chunks)),
            dma((chunks,)), dma((chunks,)),
            dma((hops, chunks)), dma((hops, chunks)),
            dma((n,)), dma((n,)), dma((n,)), dma((n,)),
            dma((hops,)), dma((hops,)), dma, dma, dma((hops,)), dma((hops,)), dma((2,)),
        ],
        compiler_params=pltpu.CompilerParams(
            collective_id=0, has_side_effects=True, vmem_limit_bytes=48 * 1024 * 1024
        ),
        cost_estimate=pl.CostEstimate(flops=flops, bytes_accessed=10 * 2**20, transcendentals=0),
    )(orbitals, potential.reshape(nz, 1, area), jnp.asarray(in_plane_matrix(area)))
    return every, corr.reshape(nb * width, nb * width)


def rotate_kernel(
    s_ref, every_ref, corr_out, out_ref, inverse, tile, spread, panel, every, sems
):
    fetch = pltpu.make_async_copy(every_ref, every, sems.at[0])
    fetch.start()
    store = pltpu.make_async_copy(s_ref, corr_out, sems.at[1])
    store.start()
    inverse_factor_in(s_ref, inverse, tile, spread, panel)
    fetch.wait()
    nz, width, _ = out_ref.shape
    b = lax.axis_index("band")

    def plane(z, carry):
        own = inverse[pl.ds(pl.multiple_of(b * width, width), width), :]
        out_ref[z] = jnp.dot(
            own, every[z], precision=EXACT, preferred_element_type=jnp.float32
        )
        return carry

    lax.fori_loop(0, nz, plane, 0)
    store.wait()


def factor_and_rotate(correlation, every, width):
    size = correlation.shape[0]
    nz, _, area = every.shape
    f32 = jnp.float32
    return pl.pallas_call(
        rotate_kernel,
        out_shape=(
            jax.ShapeDtypeStruct((size, size), f32),
            jax.ShapeDtypeStruct((nz, width, area), f32),
        ),
        in_specs=[pl.BlockSpec(memory_space=pltpu.VMEM), pl.BlockSpec(memory_space=pl.ANY)],
        out_specs=(pl.BlockSpec(memory_space=pl.ANY), pl.BlockSpec(memory_space=pltpu.VMEM)),
        scratch_shapes=[
            pltpu.VMEM((size, size), f32),
            pltpu.VMEM((BLOCK, BLOCK), f32),
            pltpu.VMEM((ROWS * ROWS, BLOCK), f32),
            pltpu.VMEM((BLOCK, size), f32),
            pltpu.VMEM((nz, size, area), f32),
            pltpu.SemaphoreType.DMA((2,)),
        ],
        compiler_params=pltpu.CompilerParams(vmem_limit_bytes=48 * 1024 * 1024),
    )(correlation, every)


def per_device(orbitals, potential):
    every, correlation = filter_and_correlate(orbitals, potential)
    correlation, rotated = factor_and_rotate(correlation, every, orbitals.shape[1])
    return (rotated, correlation)


def solution(mesh):
    return jax.shard_map(
        per_device,
        mesh=mesh,
        in_specs=(P("space", "band", None), P("space", None)),
        out_specs=(P("space", "band", None), P()),
        check_vma=False,
    )
```

time: 280 us -> 113 us (0.40)
  waiting for transfers between devices: 199 us -> 0 us
  Pallas kernels: 18 us -> 107 us
  matrix products: 33.9 us -> 0 us
  between operations: 13.8 us -> 0.65 us
  starting transfers between devices: 11.3 us -> 0 us
    pallas_call x1 -> x2, Pallas kernels: 18 us -> 107 us  [the longest x1 82.9 us: filter_and_correlate(): pl.pallas_call(functools.partial(filter_kernel, n, nb, float(nz * n * are...]
    psum x1 -> x0, waiting for transfers between devices: 70.5 us -> none  [per_device(): column_sum = lax.psum(column_part, 'space')]
    all_gather x2 -> x0, waiting for transfers between devices: 65 us -> none  [the longest x1 47.2 us: per_device(): every = lax.all_gather(second, 'band', axis=1, tiled=True)]
    ppermute x4 -> x0, waiting for transfers between devices: 63.8 us -> none  [the longest x2 63.5 us: padded(): high = lax.ppermute(block[:width], axis, backward)]
    dot_general x4 -> x0, matrix products: 33.9 us -> none  [the longest x1 12.7 us: per_device(): column_part = jnp.einsum('zig,zjg->ij', every, second, precision=EXACT)]
    ppermute x4 -> x0, starting transfers between devices: 11 us -> none  [the longest x2 11 us: padded(): high = lax.ppermute(block[:width], axis, backward)]
  transfers between devices with their start and end apart: 7 -> 0, of which waited for: 7 -> 0; matrix products, arithmetic and copies ran while one was open for 0% -> 0% of each run, Pallas kernels for 0% -> 0%
where the time goes in v1:
time: 113 us; the launch traced here: 111 us
  Pallas kernels  107 us (95%)
  local copies, waits for them, and re-layouts  3.08 us (3%)
    pallas_call x1, Pallas kernels, filter_and_correlate(): pl.pallas_call(functools.partial(filter_kernel, n, nb, float(nz * n * are...  82.9 us
    pallas_call x1, Pallas kernels, factor_and_rotate(): pl.pallas_call(rotate_kernel, out_shape=(jax.ShapeDtypeStruct((size, size...  24.6 us
    unnamed x4, local copies, waits for them, and re-layouts  2.35 us

profile of v1, /device:TPU:0, one launch (start us, length us, event | category | flops | bytes accessed | tf_op | source)
XLA Modules:
  0.0 111.2 jit_solution(5310658071363299732)
XLA Ops:
  0.6 0.7 reshape.10.p_ref
  1.4 0.0 copy-start
  1.4 1.4 %copy-done = f32[12,128,256]{2,1,0:T(8,128)S(1)} copy-done((f32[12,128,256]{2,1,0:T(8,128)S(1)}, f32[12,128,256]{2,1,0:T(8,128)}, u32[]{:S(2)}) %copy-start) | copy-done | bytes 1572888
  2.8 0.0 copy-start.1
  2.8 0.9 copy-done.1
  3.7 82.9 %shard_map.50 = (f32[12,512,256]{2,1,0:T(8,128)}, f32[4,8,16,512]{3,2,1,0:T(8,128)S(1)}) custom-call(f32[12,128,256]{2,1,0:T(8,128)S(1)} %copy-done, f32[12,1,256]{2,1,0:T(1,128)S(1)} %reshape.10.p_ref, f32[256,256]{1,0:T(8,128)S(1)} %copy-done.1), custom_call_target="tpu_custom_call" | custom-call | flops 6039797760 | bytes 10485760 | tf_op jit(solution)/shard_map/pallas_call | solution.py:438
  86.6 24.6 %shard_map.51 = (f32[512,512]{1,0:T(8,128)}, f32[12,128,256]{2,1,0:T(8,128)}) custom-call(f32[512,512]{1,0:T(8,128)S(1)} %bitcast.1, f32[12,512,256]{2,1,0:T(8,128)} %get-tuple-element.7.every_ref), custom_call_target="tpu_custom_call" | custom-call | tf_op jit(solution)/shard_map/pallas_call | solution.py:502
Async XLA Ops:
  1.4 1.4 %copy-start = (f32[12,128,256]{2,1,0:T(8,128)S(1)}, f32[12,128,256]{2,1,0:T(8,128)}, u32[]{:S(2)}) copy-start(f32[12,128,256]{2,1,0:T(8,128)} %o_ref.1) | copy-start | bytes 4718596
  2.8 0.9 copy-start.1

commit v2 on v1

--- a/solution.py
+++ b/solution.py
@@ -17,19 +17,25 @@
     lane = lax.broadcasted_iota(jnp.int32, shape, 1)
     row = lax.broadcasted_iota(jnp.int32, shape, 0)
     groups = BLOCK // ROWS
+
+    def column(block, at):
+        return jnp.broadcast_to(block[:, at : at + 1], shape)
+
+    def spread_row(at):
+        return jnp.broadcast_to(spread[at : at + 1, :], shape)
+
+    below = [tile[g * ROWS : (g + 1) * ROWS, :] for g in range(groups)]
+    ahead = [column(below[0], j) for j in range(ROWS)]
     for t in range(groups):
         base = t * ROWS
+        slot = (t % 2) * 2 * ROWS * ROWS
         inside = (lane >= base) & (lane < base + ROWS)
-        panel = tile[base : base + ROWS, :]
-        below = [tile[g * ROWS : (g + 1) * ROWS, :] for g in range(t + 1, groups)]
-        cols = [
-            [jnp.broadcast_to(block[:, base + j : base + j + 1], shape) for j in range(ROWS)]
-            for block in below
-        ]
+        panel, below = below[0], below[1:]
         for j in range(ROWS):
-            spread[j * ROWS : (j + 1) * ROWS, :] = jnp.broadcast_to(
-                panel[:, base + j : base + j + 1], shape
-            )
+            spread[slot + j * ROWS : slot + (j + 1) * ROWS, :] = ahead[j]
+        cols = [[column(block, base + j) for j in range(ROWS)] for block in below]
+        if below:
+            ahead = [column(below[0], base + ROWS + j) for j in range(ROWS)]
         tile[base : base + ROWS, :] = jnp.where(
             inside, jnp.where(lane == base + row, 1.0, 0.0), panel
         )
@@ -37,7 +43,7 @@
         own = {}
         for j in range(ROWS):
             for i in range(j, ROWS):
-                own[i, j] = jnp.broadcast_to(spread[j * ROWS + i : j * ROWS + i + 1, :], shape)
+                own[i, j] = spread_row(slot + j * ROWS + i)
         line = [
             jnp.broadcast_to(tile[base + j : base + j + 1, :], shape) for j in range(ROWS)
         ]
@@ -55,11 +61,23 @@
                 for k in range(j + 1, ROWS):
                     cols[g][k] = cols[g][k] - cols[g][j] * own[k, j]
                 below[g] = below[g] - cols[g][j] * line[j]
+            if below:
+                start = slot + (ROWS + j) * ROWS
+                spread[start : start + ROWS, :] = cols[0][j]
+                for k in range(ROWS):
+                    ahead[k] = ahead[k] - cols[0][j] * spread_row(start + k)
         for j in range(ROWS):
             tile[base + j : base + j + 1, :] = line[j][0:1, :]
-        for g in range(len(below)):
-            start = (t + 1 + g) * ROWS
-            tile[start : start + ROWS, :] = below[g]
+
+
+def split(value):
+    high = value.astype(jnp.bfloat16)
+    return high, (value - high.astype(jnp.float32)).astype(jnp.bfloat16)
+
+
+def plain_dot(left, right):
+    return jnp.dot(left, right, preferred_element_type=jnp.float32)
+
 
 COEFS = [12.0 / 7.0, -15.0 / 56.0, 10.0 / 189.0, -1.0 / 112.0, 2.0 / 1925.0, -1.0 / 16632.0]
 CENTER_COEF = -5369.0 / 1800.0
@@ -68,7 +86,7 @@
 HALF_SPAN = 38.0
 NY = 16
 REACH = 6
-CHUNK = 16
+CHUNK = 8
 MESH = pl.DeviceIdType.MESH
 
 
@@ -134,7 +152,7 @@
 
 
 def filter_kernel(
-    n, nb, cells, o_ref, p_ref, m_ref, every_out, corr_out,
+    n, nb, cells, o_ref, p_hbm, m_hbm, every_out, corr_out, p_ref, m_ref, mh_ref, ml_ref,
     ext, pot, first, mixed, every, part, inbox, corr,
     own_sem, pot_send, pot_recv, near_send, near_recv, far_send, far_recv,
     chip_send, chip_recv, core_send, core_recv, pass_send, pass_recv,
@@ -161,6 +179,10 @@
     def band_at(d):
         return lax.rem(chip + d + chips, chips) * 2 + core
 
+    fetch_p = pltpu.make_async_copy(p_hbm, p_ref, own_sem.at[1])
+    fetch_m = pltpu.make_async_copy(m_hbm, m_ref, own_sem.at[2])
+    fetch_p.start()
+    fetch_m.start()
     barrier = pltpu.get_barrier_semaphore()
     for d in range(1, n):
         pl.semaphore_signal(barrier, inc=1, device_id={"space": space_at(d)}, device_id_type=MESH)
@@ -236,13 +258,18 @@
     near_copy(0).start()
     if chunks > 1:
         near_copy(1).start()
-    own = pltpu.make_async_copy(o_ref, ext.at[pl.ds(nz, nz)], own_sem)
+    own = pltpu.make_async_copy(o_ref, ext.at[pl.ds(nz, nz)], own_sem.at[0])
     own.start()
-    up = remote(p_ref, pot.at[pl.ds(0, nz)], pot_send.at[0], pot_recv.at[0], {"space": space_at(1)})
-    down = remote(p_ref, pot.at[pl.ds(2 * nz, nz)], pot_send.at[1], pot_recv.at[1], {"space": space_at(-1)})
+    fetch_p.wait()
+    for i in range(nz):
+        pot[nz + i] = p_ref[i : i + 1, :]
+    mine = pot.at[pl.ds(nz, nz)]
+    up = remote(mine, pot.at[pl.ds(0, nz)], pot_send.at[0], pot_recv.at[0], {"space": space_at(1)})
+    down = remote(mine, pot.at[pl.ds(2 * nz, nz)], pot_send.at[1], pot_recv.at[1], {"space": space_at(-1)})
     up.start()
     down.start()
-    pot[nz : 2 * nz] = p_ref[...]
+    fetch_m.wait()
+    mh_ref[...], ml_ref[...] = split(m_ref[...])
 
     near_arrival(0).wait_recv()
     far_copy(0).start()
@@ -255,6 +282,12 @@
 
     along = [-0.5 * INV_SPACING2 * coef for coef in COEFS]
 
+    def in_plane(slab):
+        count = slab.shape[0]
+        upper, lower = split(slab)
+        both = plain_dot(jnp.concatenate([upper, lower], axis=0), mh_ref[...])
+        return both[:count] + (both[count:] + plain_dot(upper, ml_ref[...]))
+
     def do_chunk(c, carry):
         rows = rows_of(c)
 
@@ -272,9 +305,7 @@
 
         wide = nz + 2 * REACH
         slab = ext[nz - REACH : 2 * nz + REACH, rows, :].reshape(wide * CHUNK, area)
-        mixed[...] = jnp.dot(
-            slab, m_ref[...], precision=EXACT, preferred_element_type=jnp.float32
-        ).reshape(wide, CHUNK, area)
+        mixed[...] = in_plane(slab).reshape(wide, CHUNK, area)
 
         def first_plane(f, carry):
             q = f + (nz - REACH)
@@ -287,9 +318,7 @@
         lax.fori_loop(0, wide, first_plane, 0, unroll=4)
 
         slab = first[REACH : nz + REACH].reshape(nz * CHUNK, area)
-        mixed[0:nz] = jnp.dot(
-            slab, m_ref[...], precision=EXACT, preferred_element_type=jnp.float32
-        ).reshape(nz, CHUNK, area)
+        mixed[0:nz] = in_plane(slab).reshape(nz, CHUNK, area)
 
         def second_plane(j, carry):
             f = j + REACH
@@ -442,12 +471,16 @@
             jax.ShapeDtypeStruct(slices, f32),
         ),
         in_specs=[
-            pl.BlockSpec(memory_space=pl.ANY),
-            pl.BlockSpec(memory_space=pltpu.VMEM),
-            pl.BlockSpec(memory_space=pltpu.VMEM),
+            pl.BlockSpec(memory_space=pltpu.HBM),
+            pl.BlockSpec(memory_space=pltpu.HBM),
+            pl.BlockSpec(memory_space=pltpu.HBM),
         ],
-        out_specs=(pl.BlockSpec(memory_space=pl.ANY), pl.BlockSpec(memory_space=pl.ANY)),
+        out_specs=(pl.BlockSpec(memory_space=pltpu.HBM), pl.BlockSpec(memory_space=pl.ANY)),
         scratch_shapes=[
+            pltpu.VMEM((nz, area), f32),
+            pltpu.VMEM((area, area), f32),
+            pltpu.VMEM((area, area), jnp.bfloat16),
+            pltpu.VMEM((area, area), jnp.bfloat16),
             pltpu.VMEM((3 * nz, width, area), f32),
             pltpu.VMEM((3 * nz, 1, area), f32),
             pltpu.VMEM((nz + 2 * REACH, CHUNK, area), f32),
@@ -456,7 +489,7 @@
             pltpu.VMEM(slices[1:], f32),
             pltpu.VMEM(slices[1:], f32),
             pltpu.VMEM(slices, f32),
-            dma, dma((2,)), dma((2,)),
+            dma((3,)), dma((2,)), dma((2,)),
             dma((chunks,)), dma((chunks,)), dma((chunks,)), dma((chunks,)),
             dma((hops, chunks)), dma((hops, chunks)),
             dma((chunks,)), dma((chunks,)),
@@ -465,15 +498,15 @@
             dma((hops,)), dma((hops,)), dma, dma, dma((hops,)), dma((hops,)), dma((2,)),
         ],
         compiler_params=pltpu.CompilerParams(
-            collective_id=0, has_side_effects=True, vmem_limit_bytes=48 * 1024 * 1024
+            collective_id=0, has_side_effects=True, vmem_limit_bytes=60 * 1024 * 1024
         ),
         cost_estimate=pl.CostEstimate(flops=flops, bytes_accessed=10 * 2**20, transcendentals=0),
-    )(orbitals, potential.reshape(nz, 1, area), jnp.asarray(in_plane_matrix(area)))
+    )(orbitals, potential, jnp.asarray(in_plane_matrix(area)))
     return every, corr.reshape(nb * width, nb * width)
 
 
 def rotate_kernel(
-    s_ref, every_ref, corr_out, out_ref, inverse, tile, spread, panel, every, sems
+    s_ref, every_ref, corr_out, out_ref, inverse, tile, spread, panel, every, rows, sems
 ):
     fetch = pltpu.make_async_copy(every_ref, every, sems.at[0])
     fetch.start()
@@ -484,11 +517,14 @@
     nz, width, _ = out_ref.shape
     b = lax.axis_index("band")
 
+    own = split(inverse[pl.ds(pl.multiple_of(b * width, width), width), :])
+    rows[0:width] = own[0]
+    rows[width : 2 * width] = own[1]
+
     def plane(z, carry):
-        own = inverse[pl.ds(pl.multiple_of(b * width, width), width), :]
-        out_ref[z] = jnp.dot(
-            own, every[z], precision=EXACT, preferred_element_type=jnp.float32
-        )
+        upper, lower = split(every[z])
+        both = plain_dot(rows[...], upper)
+        out_ref[z] = both[:width] + (both[width:] + plain_dot(rows[0:width], lower))
         return carry
 
     lax.fori_loop(0, nz, plane, 0)
@@ -505,14 +541,15 @@
             jax.ShapeDtypeStruct((size, size), f32),
             jax.ShapeDtypeStruct((nz, width, area), f32),
         ),
-        in_specs=[pl.BlockSpec(memory_space=pltpu.VMEM), pl.BlockSpec(memory_space=pl.ANY)],
+        in_specs=[pl.BlockSpec(memory_space=pltpu.VMEM), pl.BlockSpec(memory_space=pltpu.HBM)],
         out_specs=(pl.BlockSpec(memory_space=pl.ANY), pl.BlockSpec(memory_space=pltpu.VMEM)),
         scratch_shapes=[
             pltpu.VMEM((size, size), f32),
             pltpu.VMEM((BLOCK, BLOCK), f32),
-            pltpu.VMEM((ROWS * ROWS, BLOCK), f32),
+            pltpu.VMEM((4 * ROWS * ROWS, BLOCK), f32),
             pltpu.VMEM((BLOCK, size), f32),
             pltpu.VMEM((nz, size, area), f32),
+            pltpu.VMEM((2 * width, size), jnp.bfloat16),
             pltpu.SemaphoreType.DMA((2,)),
         ],
         compiler_params=pltpu.CompilerParams(vmem_limit_bytes=48 * 1024 * 1024),

time: 113 us -> 113 us (level)
  Pallas kernels: 107 us -> 110 us
  local copies, waits for them, and re-layouts: 3.08 us -> 1.22 us
    pallas_call x1, Pallas kernels: 82.9 us -> 89.9 us  [filter_and_correlate(): pl.pallas_call(functools.partial(filter_kernel, n, nb, float(nz * n * are...]
    pallas_call x1, Pallas kernels: 24.6 us -> 20.4 us  [factor_and_rotate(): pl.pallas_call(rotate_kernel, out_shape=(jax.ShapeDtypeStruct((size, size...]
    unnamed x4 -> x2, local copies, waits for them, and re-layouts: 2.35 us -> 1.22 us
where the time goes in v2:
time: 113 us; the launch traced here: 112 us
  Pallas kernels  110 us (97%)
  local copies, waits for them, and re-layouts  1.22 us (1%)
    pallas_call x1, Pallas kernels, filter_and_correlate(): pl.pallas_call(functools.partial(filter_kernel, n, nb, float(nz * n * are...  89.9 us
    pallas_call x1, Pallas kernels, factor_and_rotate(): pl.pallas_call(rotate_kernel, out_shape=(jax.ShapeDtypeStruct((size, size...  20.4 us

profile of v2, /device:TPU:0, one launch (start us, length us, event | category | flops | bytes accessed | tf_op | source)
XLA Modules:
  0.0 112.1 jit_solution(6521806309564631724)
XLA Ops:
  0.6 89.9 %shard_map.50 = (f32[12,512,256]{2,1,0:T(8,128)}, f32[4,8,16,512]{3,2,1,0:T(8,128)}) custom-call(f32[12,128,256]{2,1,0:T(8,128)} %o_ref.1, f32[12,256]{1,0:T(8,128)} %p_hbm.1, f32[256,256]{1,0:T(8,128)} %constant.2.clone.m_hbm), custom_call_target="tpu_custom_call" | custom-call | flops 6039797760 | bytes 10485760 | tf_op jit(solution)/shard_map/pallas_call | solution.py:467
  90.5 0.0 copy-start
  90.5 1.2 %copy-done = f32[4,8,16,512]{3,2,1,0:T(8,128)S(1)} copy-done((f32[4,8,16,512]{3,2,1,0:T(8,128)S(1)}, f32[4,8,16,512]{3,2,1,0:T(8,128)}, u32[]{:S(2)}) %copy-start) | copy-done | bytes 1048600
  91.8 20.4 %shard_map.51 = (f32[512,512]{1,0:T(8,128)}, f32[12,128,256]{2,1,0:T(8,128)}) custom-call(f32[512,512]{1,0:T(8,128)S(1)} %bitcast.1, f32[12,512,256]{2,1,0:T(8,128)} %get-tuple-element.7.every_ref), custom_call_target="tpu_custom_call" | custom-call | tf_op jit(solution)/shard_map/pallas_call | solution.py:538
Async XLA Ops:
  90.5 1.2 %copy-start = (f32[4,8,16,512]{3,2,1,0:T(8,128)S(1)}, f32[4,8,16,512]{3,2,1,0:T(8,128)}, u32[]{:S(2)}) copy-start(f32[4,8,16,512]{3,2,1,0:T(8,128)} %get-tuple-element.6) | copy-start | bytes 3145732
